TPU v7x, 512 devices: a whole 4x4x16 slice. The times are simulated.
512 devices in a mesh: seq: 8 (over y, core), dp: 64 (over z, x).
Axes of the slice: x: 4, y: 4, z: 16, core: 2. Of those that a mesh axis runs over, the one named last changes fastest.
Arguments:
- frames: bfloat16 [128, 512, 1024], P('dp', 'seq'), may hold values from -6 to 6
- lengths: int32 [128], P('dp'), may hold values from 128 to 512, as said below
- w_qkv: bfloat16 [1024, 3072], P('dp'), may hold values from -4 to 4
- w_out: bfloat16 [1024, 1024], P('dp'), may hold values from -0.1875 to 0.1875
- w_point: bfloat16 [1024, 1024], P('dp'), may hold values from -0.1875 to 0.1875
- w_depth: float32 [9, 1024], replicated, may hold values from -2 to 2
Outputs:
- layer_out: bfloat16 [128, 512, 1024], P('dp', 'seq')
Inputs may be any that keep to these rules, and one draw needn't show every extreme that they name: `lengths`: every recording has at least 128 valid frames; some recording fills all 512.
All inputs are finite; a program needn't handle non-finite values.
Results may differ from a plain program's by a relative error of at most 0.014.
Values may be sent and summed in bfloat16 or wider, within the bound.
A program may use at most 64 MiB of HBM per device.

v0:
```python
import jax
import jax.numpy as jnp
from jax import lax
from jax.sharding import PartitionSpec as P

D = 1024
HEADS = 8
KERNEL = 9
HDIM = 128


def with_halo(cells, sides, width):
    for axis, dim in sides:
        count = lax.axis_size(axis)
        ends = count - 1
        head = lax.slice_in_dim(cells, 0, width, axis=dim)
        tail = lax.slice_in_dim(cells, cells.shape[dim] - width, cells.shape[dim], axis=dim)
        cells = jnp.concatenate(
            [
                lax.ppermute(tail, axis, [(i, (i + 1) % count) for i in range(ends)]),
                cells,
                lax.ppermute(head, axis, [((i + 1) % count, i) for i in range(ends)]),
            ],
            axis=dim,
        )
    return cells


def norm_rows(values):
    centre = jnp.mean(values, axis=-1, keepdims=True)
    spread = jnp.mean(jnp.square(values - centre), axis=-1, keepdims=True)
    return (values - centre) * lax.rsqrt(spread + 1e-05)


def attend(packed, length):
    total_rows = packed.shape[0]
    queries = packed[:, 0]
    keys_all = packed[:, 1]
    values_all = packed[:, 2]
    scaling = packed.shape[-1] ** (-0.5)
    block = min(512, total_rows)
    keep_mask = jnp.arange(total_rows) < length
    query_blocks = queries.reshape(total_rows // block, block, queries.shape[1], queries.shape[2])

    def one_block(qblock):
        scores = (
            jnp.einsum("qnd,knd->nqk", qblock, keys_all, preferred_element_type=jnp.float32)
            * scaling
        )
        scores = jnp.where(keep_mask[None, None, :], scores, -1e30)
        highest = jnp.max(scores, axis=-1, keepdims=True)
        powers = jnp.exp(scores - highest)
        totals = jnp.sum(powers, axis=-1, keepdims=True)
        probs = (powers / totals).astype(jnp.bfloat16)
        mixed = jnp.einsum("nqk,knd->qnd", probs, values_all, preferred_element_type=jnp.float32)
        return mixed.astype(jnp.bfloat16)

    return lax.map(one_block, query_blocks).reshape(total_rows, queries.shape[1], queries.shape[2])


def attend_many(packed, lengths):

    def one_recording(pair):
        return attend(pair[0], pair[1])

    return lax.map(one_recording, (packed, lengths))


def add_rows(left, piece):
    return jnp.dot(left, piece, preferred_element_type=jnp.float32)


def body(frames, lengths, w_qkv, w_out, w_point, w_depth):
    count = frames.shape[0]
    rows_here = frames.shape[1]
    seq_size = lax.axis_size("seq")
    per_device = HEADS // seq_size
    flat_rows = count * rows_here
    local = frames.reshape(flat_rows, D)
    normed = norm_rows(local.astype(jnp.float32)).astype(jnp.bfloat16)
    qkv = add_rows(normed, lax.all_gather(w_qkv, "dp", axis=0, tiled=True))
    qkv = qkv.astype(jnp.bfloat16).reshape(count, rows_here, 3, seq_size, per_device, HDIM)
    received = lax.all_to_all(qkv, "seq", split_axis=3, concat_axis=1, tiled=True)
    some = received.shape[4]
    packed = received.reshape(count, received.shape[1], 3, some, HDIM)
    mixed = attend_many(packed, lengths)
    heads_out = mixed.reshape(count, received.shape[1], 1, some, HDIM)
    attended = lax.all_to_all(heads_out, "seq", split_axis=1, concat_axis=2, tiled=True).reshape(
        flat_rows, D
    )
    projected = add_rows(attended, lax.all_gather(w_out, "dp", axis=0, tiled=True))
    resid = (local.astype(jnp.float32) + projected).astype(jnp.bfloat16)
    position = lax.axis_index("seq") * rows_here + jnp.arange(rows_here)
    valid = (position[None, :] < lengths[:, None]).reshape(flat_rows, 1)
    conv_in = jnp.where(valid, norm_rows(resid.astype(jnp.float32)), 0.0).astype(jnp.bfloat16)
    conv_in = conv_in.reshape(count, rows_here, D)
    padded = with_halo(conv_in, (("seq", 1),), KERNEL // 2).astype(jnp.float32)
    depth = jnp.zeros((count, rows_here, D), jnp.float32)
    for offset in range(KERNEL):
        depth = depth + padded[:, offset : offset + rows_here] * w_depth[offset]
    gated = (depth * jax.nn.sigmoid(depth)).astype(jnp.bfloat16).reshape(flat_rows, D)
    pointed = add_rows(gated, lax.all_gather(w_point, "dp", axis=0, tiled=True))
    result = jnp.where(valid, resid.astype(jnp.float32) + pointed, 0.0).astype(jnp.bfloat16)
    return result.reshape(count, rows_here, D)


def solution(mesh):
    in_specs = (P("dp", "seq", None), P("dp"), P("dp", None), P("dp", None), P("dp", None), P())
    out_specs = P("dp", "seq", None)
    return jax.shard_map(body, mesh=mesh, in_specs=in_specs, out_specs=out_specs, check_vma=False)
```

profile of v0, /device:TPU:1, one launch (start us, length us, event | category | flops | bytes accessed | tf_op | source)
XLA Modules:
  0.0 446.9 jit_solution(9650559894608089350)
XLA Ops:
  6.5 0.7 all-gather.4.cloned.1.call-update
  7.3 0.7 all-gather.6.cloned.1.call-update
  8.0 1.1 convert_reduce_fusion
  9.2 1.2 multiply_reduce_fusion.1
  10.4 1.2 fusion.18
  11.6 148.2 %all-gather.4.cloned.1.call-done = bf16[1024,3072]{1,0:T(8,128)(2,1)} async-done(((bf16[16,3072]{1,0:T(8,128)(2,1)}), bf16[1024,3072]{1,0:T(8,128)(2,1)}) %all-gather.4.cloned.1.call-update) | async-done | bytes 6291472 | tf_op jit(solution)/shard_map/all_gather | solution.py:81
  159.8 3.8 fusion.4
  163.8 1.1 copy.12
  164.9 12.4 %all-to-all-start = ((bf16[2,64,3,8,1,128]{5,1,2,0,4,3:T(8,128)(2,1)}), bf16[2,64,3,8,1,128]{5,1,2,0,4,3:T(8,128)(2,1)S(1)}, u32[]{:S(2)}, u32[]{:S(2)}) async-start(bf16[2,64,3,8,1,128]{5,1,2,0,4,3:T(8,128)(2,1)} %copy.12), calls=%async_computation | async-start | bytes 1572864 | tf_op jit(solution)/shard_map/all_to_all | solution.py:83
  177.3 0.7 all-gather.8.cloned.1.call-update
  178.1 11.6 %all-to-all-done = bf16[2,64,3,8,1,128]{5,1,2,0,4,3:T(8,128)(2,1)S(1)} async-done(((bf16[2,64,3,8,1,128]{5,1,2,0,4,3:T(8,128)(2,1)}), bf16[2,64,3,8,1,128]{5,1,2,0,4,3:T(8,128)(2,1)S(1)}, u32[]{:S(2)}, u32[]{:S(2)}) %all-to-all-start) | async-done | bytes 786464 | tf_op jit(solution)/shard_map/all_to_all | solution.py:83
  189.7 4.2 while.10
  189.7 0.6 dynamic_slice.15
  193.9 0.9 copy.15
  194.7 4.2 all-to-all-start.1
  199.1 6.4 %all-to-all-done.1 = bf16[2,512,1,1,128]{4,0,3,2,1:T(2,128)(2,1)S(1)} async-done(((bf16[2,512,1,1,128]{4,0,3,2,1:T(2,128)(2,1)}), bf16[2,512,1,1,128]{4,0,3,2,1:T(2,128)(2,1)S(1)}, u32[]{:S(2)}, u32[]{:S(2)}) %all-to-all-start.1) | async-done | bytes 262176 | tf_op jit(solution)/shard_map/all_to_all | solution.py:88
  205.7 92.0 %all-gather.6.cloned.1.call-done = bf16[1024,1024]{1,0:T(8,128)(2,1)} async-done(((bf16[16,1024]{1,0:T(8,128)(2,1)}), bf16[1024,1024]{1,0:T(8,128)(2,1)}) %all-gather.6.cloned.1.call-update) | async-done | bytes 2097168 | tf_op jit(solution)/shard_map/all_gather | solution.py:91
  297.7 2.1 fusion.24
  300.3 12.6 %collective-permute-start = (bf16[2,4,1024]{2,1,0:T(4,128)(2,1)S(1)}, bf16[2,4,1024]{2,1,0:T(4,128)(2,1)S(1)}, u32[]{:S(2)}, u32[]{:S(2)}) collective-permute-start(bf16[2,4,1024]{2,1,0:T(4,128)(2,1)S(1)} %get-tuple-element.64), channel_id=1, source_target_pairs={{0,64},{64,128},{128,192},{192,256},{256,320},{320,384},{384,448},... | collective-permute-start | bytes 49160 | tf_op jit(solution)/shard_map/ppermute | solution.py:20
  312.8 1.9 collective-permute-start.1
  314.8 3.1 collective-permute-done.1
  318.0 0.6 multiply_convert_fusion
  318.6 119.0 %all-gather.8.cloned.1.call-done = bf16[1024,1024]{1,0:T(8,128)(2,1)} async-done(((bf16[16,1024]{1,0:T(8,128)(2,1)}), bf16[1024,1024]{1,0:T(8,128)(2,1)}) %all-gather.8.cloned.1.call-update) | async-done | bytes 2097168 | tf_op jit(solution)/shard_map/all_gather | solution.py:102
  437.6 2.7 fusion.6
  (40 shorter events, 4.8 us)
Async XLA Ops:
  6.5 153.3 %all-gather.4.cloned.1.call-start = ((), (), s32[]{:S(2)}) async-start(), calls=%async_computation.2 | async-start | bytes 6389760 | tf_op jit(solution)/shard_map/all_gather | solution.py:81
  7.3 290.4 %all-gather.6.cloned.1.call-start = ((), (), s32[]{:S(2)}) async-start(), calls=%async_computation.3 | async-start | bytes 2129920 | tf_op jit(solution)/shard_map/all_gather | solution.py:91
  163.8 25.9 %copy-start.2 = (s32[2]{0:T(128)S(1)}, s32[2]{0:T(128)}, u32[]{:S(2)}) copy-start(s32[2]{0:T(128)} %param.9) | copy-start | bytes 28
  164.9 24.7 %all-to-all-start = ((bf16[2,64,3,8,1,128]{5,1,2,0,4,3:T(8,128)(2,1)}), bf16[2,64,3,8,1,128]{5,1,2,0,4,3:T(8,128)(2,1)S(1)}, u32[]{:S(2)}, u32[]{:S(2)}) async-start(bf16[2,64,3,8,1,128]{5,1,2,0,4,3:T(8,128)(2,1)} %copy.12), calls=%async_computation | async-start | bytes 1572864 | tf_op jit(solution)/shard_map/all_to_all | solution.py:83
  177.3 260.3 %all-gather.8.cloned.1.call-start = ((), (), s32[]{:S(2)}) async-start(), calls=%async_computation.4 | async-start | bytes 2129920 | tf_op jit(solution)/shard_map/all_gather | solution.py:102
  193.8 103.9 %copy-start = (bf16[2,64,1024]{2,1,0:T(8,128)(2,1)S(1)}, bf16[2,64,1024]{2,1,0:T(8,128)(2,1)}, u32[]{:S(2)}) copy-start(bf16[2,64,1024]{2,1,0:T(8,128)(2,1)} %param.8) | copy-start | bytes 786436
  194.7 10.7 %all-to-all-start.1 = ((bf16[2,512,1,1,128]{4,0,3,2,1:T(2,128)(2,1)}), bf16[2,512,1,1,128]{4,0,3,2,1:T(2,128)(2,1)S(1)}, u32[]{:S(2)}, u32[]{:S(2)}) async-start(bf16[2,512,1,1,128]{4,0,3,2,1:T(2,128)(2,1)} %bitcast.13), calls=%async_computation.1 | async-start | bytes 524288 | tf_op jit(solution)/shard_map/all_to_all | solution.py:88
  297.7 17.1 %copy-start.1 = (f32[9,1024]{1,0:T(8,128)S(1)}, f32[9,1024]{1,0:T(8,128)}, u32[]{:S(2)}) copy-start(f32[9,1024]{1,0:T(8,128)} %param.13) | copy-start | bytes 110596
  300.3 14.5 %collective-permute-start = (bf16[2,4,1024]{2,1,0:T(4,128)(2,1)S(1)}, bf16[2,4,1024]{2,1,0:T(4,128)(2,1)S(1)}, u32[]{:S(2)}, u32[]{:S(2)}) collective-permute-start(bf16[2,4,1024]{2,1,0:T(4,128)(2,1)S(1)} %get-tuple-element.64), channel_id=1, source_target_pairs={{0,64},{64,128},{128,192},{192,256},{256,320},{320,384},{384,448},... | collective-permute-start | bytes 49160 | tf_op jit(solution)/shard_map/ppermute | solution.py:20
  312.8 5.1 %collective-permute-start.1 = (bf16[2,4,1024]{2,1,0:T(4,128)(2,1)S(1)}, bf16[2,4,1024]{2,1,0:T(4,128)(2,1)S(1)}, u32[]{:S(2)}, u32[]{:S(2)}) collective-permute-start(bf16[2,4,1024]{2,1,0:T(4,128)(2,1)S(1)} %get-tuple-element.65), channel_id=1, source_target_pairs={{64,0},{128,64},{192,128},{256,192},{320,256},{384,320},{448,384},... | collective-permute-start | bytes 49160 | tf_op jit(solution)/shard_map/ppermute | solution.py:22
Sparse Core Ops, SparseCore 0:
  10.3 149.4 all-gather.3
  162.8 134.8 all-gather.5
  300.6 136.9 all-gather.7
where the time goes:
time: 455 us; the launch traced here: 447 us
  waiting for transfers between devices  382 us (84%)
  starting transfers between devices  31.1 us (7%)
  between operations  13.3 us (3%)
  matrix products  10 us (2%)
  other arithmetic  6.13 us (1%)
    all_gather x1, waiting for transfers between devices, body(): qkv = add_rows(normed, lax.all_gather(w_qkv, 'dp', axis=0, tiled=True))  148 us
    all_gather x1, waiting for transfers between devices, body(): pointed = add_rows(gated, lax.all_gather(w_point, 'dp', axis=0, tiled=True))  119 us
    all_gather x1, waiting for transfers between devices, body(): lax.all_gather(w_out, 'dp', axis=0, tiled=True)  92 us
    ppermute x1, starting transfers between devices, with_halo(): lax.ppermute(tail, axis, [(i, (i + 1) % count) for i in range(ends)])  12.6 us
    all_to_all x1, starting transfers between devices, body(): lax.all_to_all(qkv, 'seq', split_axis=3, concat_axis=1, tiled=True)  12.4 us
    all_to_all x1, waiting for transfers between devices, body(): lax.all_to_all(qkv, 'seq', split_axis=3, concat_axis=1, tiled=True)  11.6 us
  transfers between devices with their start and end apart: 7, of which 6 were waited for; matrix products, arithmetic and copies ran while one was open for 4% of the time, Pallas kernels for 0%

commit v1 on v0

v1 whole, which is shorter than its diff:
```python
import jax
import jax.numpy as jnp
from jax import lax
from jax.experimental import pallas as pl
from jax.experimental.pallas import tpu as pltpu
from jax.sharding import PartitionSpec as P

D = 1024
HEADS = 8
KERNEL = 9
HDIM = 128
LEN = 512
HALO = 16
MESH = pl.DeviceIdType.MESH
LOG2E = 1.4426950408889634
N_SEM = 96


def norm_rows(values):
    centre = jnp.mean(values, axis=-1, keepdims=True)
    moved = values - centre
    spread = jnp.mean(jnp.square(moved), axis=-1, keepdims=True)
    return moved * lax.rsqrt(spread + 1e-05)


def kernel(
    len_ref, fr_ref, wq_ref, wo_ref, wp_ref, wd_ref, out_ref,
    NB, FH, BW, BO, BP, QKV, ATT, A, CV, ssem, rsem,
):
    s = lax.axis_index("seq")
    d = lax.axis_index("dp")
    y, c = s // 2, s % 2
    z, x = d // 4, d % 4
    j, r = z // 4, z % 4

    def at_z(k):
        return {"seq": s, "dp": lax.rem(z + k + 16, 16) * 4 + x}

    def at_x(k):
        return {"seq": s, "dp": z * 4 + lax.rem(x + k, 4)}

    def at_y(k):
        return {"seq": lax.rem(y + k, 4) * 2 + c, "dp": d}

    def at_s(k):
        return {"seq": lax.rem(s + k, 8), "dp": d}

    sibling = {"seq": y * 2 + 1 - c, "dp": d}

    started = []

    def copy(src, dst, device):
        n = len(started)
        made = pltpu.make_async_remote_copy(
            src_ref=src, dst_ref=dst, send_sem=ssem.at[n], recv_sem=rsem.at[n],
            device_id=device, device_id_type=MESH,
        )
        made.start()
        started.append(made)
        return made

    def same(ref, device):
        return copy(ref, ref, device)

    def arrived(copies):
        for one in copies:
            one.wait_recv()

    barrier = pltpu.get_barrier_semaphore()
    peers = [at_z(k) for k in (1, -1, 2, -2, 4, -4, 8)]
    peers += [at_x(k) for k in (1, 2, 3)] + [at_s(k) for k in range(1, 8)]
    for peer in peers:
        pl.semaphore_signal(barrier, inc=1, device_id=peer, device_id_type=MESH)

    def cols(ref, start, size):
        return ref[:, pl.ds(pl.multiple_of(start, 128), size)]

    def lanes(start, size):
        return pl.ds(pl.multiple_of(start, 128), size)

    for part in range(3):
        BW[j, r, x, :, part * 128 : part * 128 + 128] = cols(wq_ref, part * D + s * 128, 128)
    half = lanes(c * 512, 512)
    eighth = lanes(s * 128, 128)
    BO[j, r, x, :, half] = cols(wo_ref, c * 512, 512)
    BP[j, r, x, :, eighth] = cols(wp_ref, s * 128, 128)
    pl.semaphore_wait(barrier, len(peers))

    def hubs(ref):
        return [same(ref, at_z(k)) for k in (4, -4, 8)]

    def near(get):
        every, low, high = get(slice(None)), get(slice(0, 2)), get(slice(2, 4))
        return [same(every, at_z(1)), same(every, at_z(-1)), same(low, at_z(2)), same(high, at_z(-2))]

    def across(ref):
        return [same(ref, at_x(k)) for k in (1, 3, 2)]

    qk = slice(0, 256)
    vv = slice(256, 384)
    v1 = across(BW.at[j, r, x, :, vv])
    q1 = hubs(BW.at[j, r, x, :, qk])

    local = fr_ref[...].astype(jnp.float32)
    NB[:, s] = norm_rows(local).astype(jnp.bfloat16)
    own = NB.at[:, s]
    f1 = [same(own, at_y(1)), same(own, at_y(3)), same(own, sibling), same(own, at_y(2))]
    h1 = [
        copy(fr_ref.at[:, 64 - HALO : 64], FH.at[:, 0:HALO], at_s(1)),
        copy(fr_ref.at[:, 0:HALO], FH.at[:, 64 + HALO : 64 + 2 * HALO], at_s(7)),
    ]
    FH[:, HALO : 64 + HALO] = fr_ref[...]

    arrived(v1)
    v2 = hubs(BW.at[j, r, :, :, vv])
    arrived(q1)
    q2 = near(lambda js: BW.at[js, r, x, :, qk])
    p1 = hubs(BP.at[j, r, x, :, eighth])
    o1 = hubs(BO.at[j, r, x, :, half])
    arrived(v2)
    v3 = near(lambda js: BW.at[js, r, :, :, vv])
    arrived(q2)
    q3 = across(BW.at[:, :, x, :, qk])
    arrived(p1)
    p2 = near(lambda js: BP.at[js, r, x, :, eighth])
    arrived(o1)
    o2 = near(lambda js: BO.at[js, r, x, :, half])
    g1 = []
    for k, one in ((3, f1[0]), (1, f1[1]), (2, f1[3])):
        one.wait_recv()
        there = lax.rem(y + k, 4) * 2 + c
        g1.append(same(NB.at[:, there], sibling))
    arrived(p2)
    p3 = across(BP.at[:, :, x, :, eighth])
    arrived(q3)
    arrived(v3)
    arrived(o2)
    o3 = across(BO.at[:, :, x, :, half])
    k1 = [same(BO.at[:, :, x, :, half], sibling)]
    arrived([f1[2]])
    arrived(g1)

    weight = BW[...].reshape(D, 3 * HDIM)
    for rec in range(2):
        rows = NB[rec].reshape(LEN, D)
        QKV[rec] = jnp.dot(rows, weight, preferred_element_type=jnp.float32).astype(jnp.bfloat16)
    arrived(p3)
    p4 = [same(BP.at[:, :, :, :, eighth], at_y(k)) for k in (1, 3, 2)]
    k2 = [same(BP.at[:, :, :, :, eighth], sibling)]

    a1 = []
    zeros = jnp.zeros((2, HALO, HDIM), jnp.bfloat16)
    ATT[:, 0:HALO] = zeros
    ATT[:, LEN + HALO : LEN + 2 * HALO] = zeros
    key_at = lax.broadcasted_iota(jnp.int32, (128, LEN), 1)
    for rec in range(2):
        keep = key_at < len_ref[rec]
        keys = QKV[rec, :, HDIM : 2 * HDIM]
        vals = QKV[rec, :, 2 * HDIM : 3 * HDIM]
        for part in range(4):
            query = QKV[rec, part * 128 : part * 128 + 128, 0:HDIM]
            scores = lax.dot_general(
                query, keys, (((1,), (1,)), ((), ())), preferred_element_type=jnp.float32
            )
            scores = jnp.where(keep, scores, -1e30)
            highest = jnp.max(scores, axis=-1, keepdims=True)
            powers = jnp.exp2((scores - highest) * (LOG2E * HDIM**-0.5))
            totals = jnp.sum(powers, axis=-1, keepdims=True)
            mixed = jnp.dot(powers.astype(jnp.bfloat16), vals, preferred_element_type=jnp.float32)
            ATT[rec, HALO + part * 128 : HALO + part * 128 + 128] = (mixed / totals).astype(
                jnp.bfloat16
            )
        for k in (4, 3, 5, 2, 6, 1, 7):
            there = lax.rem(s + k, 8)
            src = ATT.at[rec, pl.ds(pl.multiple_of(there * 64, 64), 64 + 2 * HALO)]
            a1.append(copy(src, A.at[rec, :, eighth], at_s(k)))
        A[rec, :, eighth] = ATT[rec, pl.ds(pl.multiple_of(s * 64, 64), 64 + 2 * HALO)]

    for k, one in ((3, o3[0]), (1, o3[1]), (2, o3[2])):
        one.wait_recv()
        k1.append(same(BO.at[:, :, lax.rem(x + k, 4), :, half], sibling))
    for k, one in ((3, p4[0]), (1, p4[1]), (2, p4[2])):
        one.wait_recv()
        there = lanes((lax.rem(y + k, 4) * 2 + c) * 128, 128)
        k2.append(same(BP.at[:, :, :, :, there], sibling))
    arrived(h1)
    arrived(a1)
    arrived(k1)

    tall = 64 + 2 * HALO
    attended = A[...].reshape(2 * tall, D)
    projected = jnp.dot(attended, BO[...].reshape(D, D), preferred_element_type=jnp.float32)
    resid = (FH[...].astype(jnp.float32) + projected.reshape(2, tall, D)).astype(jnp.bfloat16)
    FH[...] = resid
    position = s * 64 - HALO + lax.broadcasted_iota(jnp.int32, (tall, 1), 0)
    inside = (position >= 0) & (position < LEN)
    for rec in range(2):
        valid = inside & (position < len_ref[rec])
        normed = jnp.where(valid, norm_rows(resid[rec].astype(jnp.float32)), 0.0)
        CV[rec] = normed.astype(jnp.bfloat16).astype(jnp.float32)
    gated = []
    for rec in range(2):
        depth = jnp.zeros((64, D), jnp.float32)
        for tap in range(KERNEL):
            start = HALO - KERNEL // 2 + tap
            depth = depth + CV[rec, start : start + 64] * wd_ref[tap : tap + 1]
        gated.append((depth * jax.nn.sigmoid(depth)).astype(jnp.bfloat16))
    gated = jnp.concatenate(gated, axis=0)
    arrived(k2)
    pointed = jnp.dot(gated, BP[...].reshape(D, D), preferred_element_type=jnp.float32)
    position = s * 64 + lax.broadcasted_iota(jnp.int32, (64, 1), 0)
    for rec in range(2):
        total = FH[rec, HALO : 64 + HALO].astype(jnp.float32) + pointed[rec * 64 : rec * 64 + 64]
        out_ref[rec] = jnp.where(position < len_ref[rec], total, 0.0).astype(jnp.bfloat16)
    for one in started:
        one.wait_send()


def body(frames, lengths, w_qkv, w_out, w_point, w_depth):
    vmem = pl.BlockSpec(memory_space=pltpu.VMEM)
    smem = pl.BlockSpec(memory_space=pltpu.SMEM)
    tall = 64 + 2 * HALO
    bf16 = jnp.bfloat16
    return pl.pallas_call(
        kernel,
        out_shape=jax.ShapeDtypeStruct((2, 64, D), bf16),
        in_specs=[smem, vmem, vmem, vmem, vmem, vmem],
        out_specs=vmem,
        scratch_shapes=[
            pltpu.VMEM((2, 8, 64, D), bf16),
            pltpu.VMEM((2, tall, D), bf16),
            pltpu.VMEM((4, 4, 4, 16, 3 * HDIM), bf16),
            pltpu.VMEM((4, 4, 4, 16, D), bf16),
            pltpu.VMEM((4, 4, 4, 16, D), bf16),
            pltpu.VMEM((2, LEN, 3 * HDIM), bf16),
            pltpu.VMEM((2, LEN + 2 * HALO, HDIM), bf16),
            pltpu.VMEM((2, tall, D), bf16),
            pltpu.VMEM((2, tall, D), jnp.float32),
            pltpu.SemaphoreType.DMA((N_SEM,)),
            pltpu.SemaphoreType.DMA((N_SEM,)),
        ],
        compiler_params=pltpu.CompilerParams(
            collective_id=0, has_side_effects=True, vmem_limit_bytes=48 << 20
        ),
        name="conformer",
    )(lengths, frames, w_qkv, w_out, w_point, w_depth)


def solution(mesh):
    in_specs = (P("dp", "seq", None), P("dp"), P("dp", None), P("dp", None), P("dp", None), P())
    out_specs = P("dp", "seq", None)
    return jax.shard_map(body, mesh=mesh, in_specs=in_specs, out_specs=out_specs, check_vma=False)
```

time: 455 us -> 66.4 us (0.15); the launches traced: 447 us -> 65.6 us
  waiting for transfers between devices: 382 us -> 0 us
  Pallas kernels: 0 us -> 60.1 us
  starting transfers between devices: 31.1 us -> 0 us
  between operations: 13.3 us -> 0.02 us
  matrix products: 10 us -> 0 us
  other arithmetic: 6.13 us -> 0 us
    all_gather x3 -> x0, waiting for transfers between devices: 359 us -> none  [the longest x1 148 us: body(): qkv = add_rows(normed, lax.all_gather(w_qkv, 'dp', axis=0, tiled=True))]
    pallas_call x0 -> x1, Pallas kernels: none -> 60.1 us  [body(): pl.pallas_call(kernel, out_shape=jax.ShapeDtypeStruct((2, 64, D), bf16),...]
    all_to_all x2 -> x0, waiting for transfers between devices: 17.9 us -> none  [the longest x1 11.6 us: body(): lax.all_to_all(qkv, 'seq', split_axis=3, concat_axis=1, tiled=True)]
    all_to_all x2 -> x0, starting transfers between devices: 16.6 us -> none  [the longest x1 12.4 us: body(): lax.all_to_all(qkv, 'seq', split_axis=3, concat_axis=1, tiled=True)]
    ppermute x2 -> x0, starting transfers between devices: 14.5 us -> none  [the longest x1 12.6 us: with_halo(): lax.ppermute(tail, axis, [(i, (i + 1) % count) for i in range(ends)])]
    dot_general x7 -> x0, matrix products: 10 us -> none  [the longest x3 8.69 us: add_rows(): return jnp.dot(left, piece, preferred_element_type=jnp.float32)]
    unnamed x7 -> x13, local copies, waits for them, and re-layouts: 0.17 us -> 5.56 us
  transfers between devices with their start and end apart: 7 -> 0, of which waited for: 6 -> 0; matrix products, arithmetic and copies ran while one was open for 4% -> 0% of each run, Pallas kernels for 0% -> 0%
where the time goes in v1:
time: 66.4 us; the launch traced here: 65.6 us
  Pallas kernels  60.1 us (91%)
  local copies, waits for them, and re-layouts  5.56 us (8%)
    pallas_call x1, Pallas kernels, body(): pl.pallas_call(kernel, out_shape=jax.ShapeDtypeStruct((2, 64, D), bf16),...  60.1 us
    unnamed x13, local copies, waits for them, and re-layouts  5.56 us

profile of v1, /device:TPU:1, one launch (start us, length us, event | category | flops | bytes accessed | tf_op | source)
XLA Modules:
  0.0 65.6 jit_solution(9862828418689642814)
XLA Ops:
  0.0 0.0 copy-start
  0.0 0.9 %copy-done = bf16[2,64,1024]{2,1,0:T(8,128)(2,1)S(1)} copy-done((bf16[2,64,1024]{2,1,0:T(8,128)(2,1)S(1)}, bf16[2,64,1024]{2,1,0:T(8,128)(2,1)}, u32[]{:S(2)}) %copy-start) | copy-done | bytes 262168
  1.0 0.0 copy-start.1
  1.0 0.9 %copy-done.1 = bf16[16,3072]{1,0:T(8,128)(2,1)S(1)} copy-done((bf16[16,3072]{1,0:T(8,128)(2,1)S(1)}, bf16[16,3072]{1,0:T(8,128)(2,1)}, u32[]{:S(2)}) %copy-start.1) | copy-done | bytes 98328
  1.8 0.0 copy-start.2
  1.8 0.8 %copy-done.2 = f32[9,1024]{1,0:T(8,128)S(1)} copy-done((f32[9,1024]{1,0:T(8,128)S(1)}, f32[9,1024]{1,0:T(8,128)}, u32[]{:S(2)}) %copy-start.2) | copy-done | bytes 36888
  2.7 0.0 copy-start.3
  2.7 0.8 %copy-done.3 = bf16[16,1024]{1,0:T(8,128)(2,1)S(1)} copy-done((bf16[16,1024]{1,0:T(8,128)(2,1)S(1)}, bf16[16,1024]{1,0:T(8,128)(2,1)}, u32[]{:S(2)}) %copy-start.3) | copy-done | bytes 32792
  3.4 0.0 copy-start.4
  3.4 0.8 %copy-done.4 = bf16[16,1024]{1,0:T(8,128)(2,1)S(1)} copy-done((bf16[16,1024]{1,0:T(8,128)(2,1)S(1)}, bf16[16,1024]{1,0:T(8,128)(2,1)}, u32[]{:S(2)}) %copy-start.4) | copy-done | bytes 32792
  4.2 0.0 copy-start.5
  4.2 0.7 copy-done.5
  4.9 60.1 %conformer.1 = bf16[2,64,1024]{2,1,0:T(8,128)(2,1)S(1)} custom-call(s32[2]{0:T(128)S(1)} %copy-done.5, bf16[2,64,1024]{2,1,0:T(8,128)(2,1)S(1)} %copy-done, bf16[16,3072]{1,0:T(8,128)(2,1)S(1)} %copy-done.1, bf16[16,1024]{1,0:T(8,128)(2,1)S(1)} %copy-done.3, bf16[16,1024]{1,0:T(8,128)(2,1)S(1)} %copy-done.4, f32[9,1024]{1,0:T(8,128)S(1)} %copy-done.2), custom_call_target="tpu_custom_call" | custom-call | tf_op jit(solution)/shard_map/conformer/pallas_call | solution.py:224
  64.9 0.7 %copy.8 = bf16[2,64,1024]{2,1,0:T(8,128)(2,1)} copy(bf16[2,64,1024]{2,1,0:T(8,128)(2,1)S(1)} %conformer.1) | data formatting | bytes 524288
Async XLA Ops:
  0.0 0.9 %copy-start = (bf16[2,64,1024]{2,1,0:T(8,128)(2,1)S(1)}, bf16[2,64,1024]{2,1,0:T(8,128)(2,1)}, u32[]{:S(2)}) copy-start(bf16[2,64,1024]{2,1,0:T(8,128)(2,1)} %fr_ref.1) | copy-start | bytes 786436
  1.0 0.9 %copy-start.1 = (bf16[16,3072]{1,0:T(8,128)(2,1)S(1)}, bf16[16,3072]{1,0:T(8,128)(2,1)}, u32[]{:S(2)}) copy-start(bf16[16,3072]{1,0:T(8,128)(2,1)} %wq_ref.1) | copy-start | bytes 294916
  1.8 0.8 %copy-start.2 = (f32[9,1024]{1,0:T(8,128)S(1)}, f32[9,1024]{1,0:T(8,128)}, u32[]{:S(2)}) copy-start(f32[9,1024]{1,0:T(8,128)} %wd_ref.1) | copy-start | bytes 110596
  2.7 0.8 %copy-start.3 = (bf16[16,1024]{1,0:T(8,128)(2,1)S(1)}, bf16[16,1024]{1,0:T(8,128)(2,1)}, u32[]{:S(2)}) copy-start(bf16[16,1024]{1,0:T(8,128)(2,1)} %wo_ref.1) | copy-start | bytes 98308
  3.4 0.8 %copy-start.4 = (bf16[16,1024]{1,0:T(8,128)(2,1)S(1)}, bf16[16,1024]{1,0:T(8,128)(2,1)}, u32[]{:S(2)}) copy-start(bf16[16,1024]{1,0:T(8,128)(2,1)} %wp_ref.1) | copy-start | bytes 98308
  4.2 0.7 copy-start.5

commit v2 on v1

v2 whole, which is shorter than its diff:
```python
import jax
import jax.numpy as jnp
from jax import lax
from jax.experimental import pallas as pl
from jax.experimental.pallas import tpu as pltpu
from jax.sharding import PartitionSpec as P

D = 1024
HEADS = 8
KERNEL = 9
HDIM = 128
LEN = 512
HALO = 16
MESH = pl.DeviceIdType.MESH
LOG2E = 1.4426950408889634
N_SEM = 160
WA = 128
RING_X = 0
RING_Y = 1
OA_AT = 2


def norm_rows(values):
    centre = jnp.mean(values, axis=-1, keepdims=True)
    moved = values - centre
    spread = jnp.mean(jnp.square(moved), axis=-1, keepdims=True)
    return moved * lax.rsqrt(spread + 1e-05)


def kernel(
    len_hbm, fr_ref, wq_ref, wo_ref, wp_ref, wd_hbm, out_ref,
    NB, FH, BW, BO, BP, QKV, ATT, A, CV, wd_ref, len_ref, ssem, rsem, lsem,
):
    s = lax.axis_index("seq")
    d = lax.axis_index("dp")
    y, c = s // 2, s % 2
    z, x = d // 4, d % 4

    def at_z(k):
        return {"seq": s, "dp": lax.rem(z + k + 16, 16) * 4 + x}

    def at_x(k):
        return {"seq": s, "dp": z * 4 + lax.rem(x + k, 4)}

    def at_y(k):
        return {"seq": lax.rem(y + k, 4) * 2 + c, "dp": d}

    def at_s(k):
        return {"seq": lax.rem(s + k, 8), "dp": d}

    sibling = {"seq": y * 2 + 1 - c, "dp": d}

    def lanes(start, size):
        return pl.ds(pl.multiple_of(start, 128), size)

    half = lanes(c * 512, 512)
    eighth = lanes(s * 128, 128)
    part_b, part_a = lanes(c * 512, 512 - WA), lanes(c * 512 + 512 - WA, WA)

    local = [(fr_ref, FH.at[:, HALO : 64 + HALO])]
    local += [
        (wq_ref.at[:, lanes(part * D + s * 128, 128)], BW.at[4, x, :, part * 128 : part * 128 + 128])
        for part in range(3)
    ]
    local += [
        (wp_ref.at[:, eighth], BP.at[4, x, :, eighth]),
        (wo_ref.at[:, half], BO.at[4, x, :, half]),
        (wd_hbm, wd_ref),
        (len_hbm, len_ref),
    ]
    local = [
        pltpu.make_async_copy(src, dst, lsem.at[i]) for i, (src, dst) in enumerate(local)
    ]
    for one in local:
        one.start()

    started = []

    def copy(src, dst, device):
        n = len(started)
        made = pltpu.make_async_remote_copy(
            src_ref=src, dst_ref=dst, send_sem=ssem.at[n], recv_sem=rsem.at[n],
            device_id=device, device_id_type=MESH,
        )
        made.start()
        started.append(made)
        return made

    def same(ref, device):
        return copy(ref, ref, device)

    def arrived(copies):
        for one in copies:
            one.wait_recv()

    barrier = pltpu.get_barrier_semaphore()
    peers = [at_z(k) for k in (4, -4, 3, -3, 2, -2, 1, -1)]
    peers += [at_x(k) for k in (2, 1, 3)] + [at_s(k) for k in (4, 3, 5, 2, 6, 1, 7)]
    for peer in peers:
        pl.semaphore_signal(barrier, inc=1, device_id=peer, device_id_type=MESH)
    for one in local:
        one.wait()
    pl.semaphore_wait(barrier, len(peers))

    def hubs(ref, at):
        own = at(ref, 4)
        return [copy(own, at(ref, 0), at_z(4)), copy(own, at(ref, 8), at_z(-4))]

    def near(ref, at):
        own = at(ref, 4)
        made = []
        for k in (3, 2, 1):
            made += [copy(own, at(ref, 4 - k), at_z(k)), copy(own, at(ref, 4 + k), at_z(-k))]
        return made

    def far(ref, at):
        low, high = at(ref, 0), at(ref, 8)
        made = [copy(at(ref, 8 * c), at(ref, 12), at_z(4 - 8 * c))]
        for k in (3, 2, 1):
            made += [copy(low, at(ref, 16 - k), at_z(k)), copy(high, at(ref, 8 + k), at_z(-k))]
        return made

    def across(ref):
        return [same(ref, at_x(k)) for k in (2, 1, 3)]

    slot = lambda ref, i: ref.at[i, x]
    slot_half = lambda ref, i: ref.at[i, x, :, part_b]
    slot_eighth = lambda ref, i: ref.at[i, x, :, eighth]
    slot_a = lambda ref, i: ref.at[i, :, :, part_a]
    NEAR, FAR = slice(0, 9), slice(9, 16)

    def ring(get, at, on=1):
        made = [same(get(0, 2), at(1)), same(get(0, 2), at(3))]
        return made if on else made + [same(get(0, 2), at(2))]

    def ring_on(get, at, first, on=1):
        first[0].wait_recv()
        made = [same(get(3, 0), at(1))] if on else [first[2]]
        first[1].wait_recv()
        return made + [same(get(1, 1), at(3))] if on else made

    def x_blocks(parts):
        return lambda k, part: BO.at[parts[part], lax.rem(x + k, 4), :, part_b]

    near_x = x_blocks((slice(0, 5), slice(5, 9), NEAR))
    far_x = x_blocks((slice(9, 12), slice(12, 16), FAR))

    def y_blocks(wave):
        parts = (slice(0, 2), slice(2, 4), slice(0, 4))
        return lambda k, part: BP.at[
            wave, parts[part], :, lanes((lax.rem(y + k, 4) * 2 + c) * 128, 128)
        ]

    near_y, far_y = y_blocks(NEAR), y_blocks(FAR)

    def frames_y(k, part):
        there = lax.rem(y + k, 4) * 2 + c
        return NB.at[part, there] if part < 2 else NB.at[:, there]

    oa0 = across(BO.at[4, x, :, part_a]) if WA else []
    oah, oan = [], []

    def oa_start(when):
        if WA and when == OA_AT:
            arrived(oa0)
            oah.extend(hubs(BO, slot_a))
            oan.extend(near(BO, slot_a))

    wh = hubs(BW, slot)
    wn = near(BW, slot)
    ph = hubs(BP, slot_eighth)
    oh = hubs(BO, slot_half)

    NB[:, s] = norm_rows(FH[:, HALO : 64 + HALO].astype(jnp.float32)).astype(jnp.bfloat16)
    f1 = ring(frames_y, at_y)
    f0 = [same(NB.at[:, s], sibling)]
    h1 = [
        copy(fr_ref.at[:, 64 - HALO : 64], FH.at[:, 0:HALO], at_s(1)),
        copy(fr_ref.at[:, 0:HALO], FH.at[:, 64 + HALO : 64 + 2 * HALO], at_s(7)),
    ]

    arrived(wh)
    wf = far(BW, slot)
    pn = near(BP, slot_eighth)
    on = near(BO, slot_half)
    arrived(wn)
    wxn = across(BW.at[NEAR, x])
    arrived(ph)
    pf = far(BP, slot_eighth)
    arrived(oh)
    of = far(BO, slot_half)
    oa_start(0)
    arrived(pn)
    pxn = across(BP.at[NEAR, x, :, eighth])
    arrived(wf)
    wxf = across(BW.at[FAR, x])
    oa_start(1)
    f2 = ring_on(frames_y, at_y, f1)
    g1 = [same(frames_y(k, 2), sibling) for k in (1, 3)]
    arrived(pf)
    pxf = across(BP.at[FAR, x, :, eighth])
    arrived(on)
    oxn = ring(near_x, at_x, RING_X)
    arrived(of)
    oxf = ring(far_x, at_x, RING_X)
    k1 = [same(BO.at[:, x, :, part_b], sibling)]
    oa_start(2)
    arrived(pxn)
    pyn = ring(near_y, at_y, RING_Y)
    arrived(f2)
    g1 += [same(frames_y(2, 2), sibling)]
    arrived(wxn)
    arrived(f0)
    arrived(g1)
    arrived(wxf)

    def natural(ref):
        planes = [ref[lax.rem(i - z + 20, 16)] for i in range(16)]
        return jnp.concatenate([p.reshape(64, p.shape[-1]) for p in planes], axis=0)

    weight = natural(BW)
    for rec in range(2):
        rows = NB[rec].reshape(LEN, D)
        QKV[rec] = jnp.dot(rows, weight, preferred_element_type=jnp.float32).astype(jnp.bfloat16)
    if WA:
        arrived(oah)
        oaf = far(BO, slot_a)
    arrived(pxf)
    pyf = ring(far_y, at_y, RING_Y)
    k2 = [same(BP.at[:, :, :, eighth], sibling)]

    a1 = []
    zeros = jnp.zeros((2, HALO, HDIM), jnp.bfloat16)
    ATT[:, 0:HALO] = zeros
    ATT[:, LEN + HALO : LEN + 2 * HALO] = zeros
    key_at = lax.broadcasted_iota(jnp.int32, (128, LEN), 1)

    def attention(rec):
        keep = key_at < len_ref[rec]
        keys = QKV[rec, :, HDIM : 2 * HDIM]
        vals = QKV[rec, :, 2 * HDIM : 3 * HDIM]
        for part in range(4):
            query = QKV[rec, part * 128 : part * 128 + 128, 0:HDIM]
            scores = lax.dot_general(
                query, keys, (((1,), (1,)), ((), ())), preferred_element_type=jnp.float32
            )
            scores = jnp.where(keep, scores, -1e30)
            highest = jnp.max(scores, axis=-1, keepdims=True)
            powers = jnp.exp2((scores - highest) * (LOG2E * HDIM**-0.5))
            totals = jnp.sum(powers, axis=-1, keepdims=True)
            mixed = jnp.dot(powers.astype(jnp.bfloat16), vals, preferred_element_type=jnp.float32)
            ATT[rec, HALO + part * 128 : HALO + part * 128 + 128] = (mixed / totals).astype(
                jnp.bfloat16
            )
        made = []
        for k in (4, 3, 5, 2, 6, 1, 7):
            there = lax.rem(s + k, 8)
            src = ATT.at[rec, pl.ds(pl.multiple_of(there * 64, 64), 64 + 2 * HALO)]
            made += [copy(src, A.at[rec, :, eighth], at_s(k))]
        A[rec, :, eighth] = ATT[rec, pl.ds(pl.multiple_of(s * 64, 64), 64 + 2 * HALO)]
        return made

    a1 += attention(0)
    oxn2 = ring_on(near_x, at_x, oxn, RING_X)
    k1 += [same(near_x(k, 2), sibling) for k in (1, 3)]
    a1 += attention(1)
    oxf2 = ring_on(far_x, at_x, oxf, RING_X)
    k1 += [same(far_x(k, 2), sibling) for k in (1, 3)]
    if WA:
        arrived(oan)
        k1 += [same(slot_a(BO, NEAR), sibling)]
    pyn2 = ring_on(near_y, at_y, pyn, RING_Y)
    k2 += [same(near_y(k, 2), sibling) for k in (1, 3)]
    arrived(oxn2)
    k1 += [same(near_x(2, 2), sibling)]
    arrived(oxf2)
    k1 += [same(far_x(2, 2), sibling)]
    if WA:
        arrived(oaf)
        k1 += [same(slot_a(BO, FAR), sibling)]
    pyf2 = ring_on(far_y, at_y, pyf, RING_Y)
    k2 += [same(far_y(k, 2), sibling) for k in (1, 3)]
    arrived(pyn2)
    k2 += [same(near_y(2, 2), sibling)]
    arrived(pyf2)
    k2 += [same(far_y(2, 2), sibling)]
    arrived(h1)
    arrived(a1)
    arrived(k1)

    tall = 64 + 2 * HALO
    attended = A[...].reshape(2 * tall, D)
    projected = jnp.dot(attended, natural(BO), preferred_element_type=jnp.float32)
    resid = (FH[...].astype(jnp.float32) + projected.reshape(2, tall, D)).astype(jnp.bfloat16)
    FH[...] = resid
    position = s * 64 - HALO + lax.broadcasted_iota(jnp.int32, (tall, 1), 0)
    inside = (position >= 0) & (position < LEN)
    for rec in range(2):
        valid = inside & (position < len_ref[rec])
        normed = jnp.where(valid, norm_rows(resid[rec].astype(jnp.float32)), 0.0)
        CV[rec] = normed.astype(jnp.bfloat16).astype(jnp.float32)
    gated = []
    for rec in range(2):
        depth = jnp.zeros((64, D), jnp.float32)
        for tap in range(KERNEL):
            start = HALO - KERNEL // 2 + tap
            depth = depth + CV[rec, start : start + 64] * wd_ref[tap : tap + 1]
        gated.append((depth * jax.nn.sigmoid(depth)).astype(jnp.bfloat16))
    gated = jnp.concatenate(gated, axis=0)
    arrived(k2)
    pointed = jnp.dot(gated, natural(BP), preferred_element_type=jnp.float32)
    position = s * 64 + lax.broadcasted_iota(jnp.int32, (64, 1), 0)
    for rec in range(2):
        total = FH[rec, HALO : 64 + HALO].astype(jnp.float32) + pointed[rec * 64 : rec * 64 + 64]
        out_ref[rec] = jnp.where(position < len_ref[rec], total, 0.0).astype(jnp.bfloat16)
    for one in started:
        one.wait_send()


def body(frames, lengths, w_qkv, w_out, w_point, w_depth):
    vmem = pl.BlockSpec(memory_space=pltpu.VMEM)
    hbm = pl.BlockSpec(memory_space=pltpu.HBM)
    tall = 64 + 2 * HALO
    bf16 = jnp.bfloat16
    return pl.pallas_call(
        kernel,
        out_shape=jax.ShapeDtypeStruct((2, 64, D), bf16),
        in_specs=[hbm] * 6,
        out_specs=vmem,
        scratch_shapes=[
            pltpu.VMEM((2, 8, 64, D), bf16),
            pltpu.VMEM((2, tall, D), bf16),
            pltpu.VMEM((16, 4, 16, 3 * HDIM), bf16),
            pltpu.VMEM((16, 4, 16, D), bf16),
            pltpu.VMEM((16, 4, 16, D), bf16),
            pltpu.VMEM((2, LEN, 3 * HDIM), bf16),
            pltpu.VMEM((2, LEN + 2 * HALO, HDIM), bf16),
            pltpu.VMEM((2, tall, D), bf16),
            pltpu.VMEM((2, tall, D), jnp.float32),
            pltpu.VMEM((KERNEL, D), jnp.float32),
            pltpu.SMEM((2,), jnp.int32),
            pltpu.SemaphoreType.DMA((N_SEM,)),
            pltpu.SemaphoreType.DMA((N_SEM,)),
            pltpu.SemaphoreType.DMA((8,)),
        ],
        compiler_params=pltpu.CompilerParams(
            collective_id=0, has_side_effects=True, vmem_limit_bytes=61 << 20
        ),
        name="conformer",
    )(lengths, frames, w_qkv, w_out, w_point, w_depth)


def solution(mesh):
    in_specs = (P("dp", "seq", None), P("dp"), P("dp", None), P("dp", None), P("dp", None), P())
    out_specs = P("dp", "seq", None)
    return jax.shard_map(body, mesh=mesh, in_specs=in_specs, out_specs=out_specs, check_vma=False)
```

time: 66.4 us -> 53.9 us (0.81)
  Pallas kernels: 60.1 us -> 52.1 us
  local copies, waits for them, and re-layouts: 5.56 us -> 1.67 us
    pallas_call x1, Pallas kernels: 60.1 us -> 52.1 us  [body(): pl.pallas_call(kernel, out_shape=jax.ShapeDtypeStruct((2, 64, D), bf16),...]
    unnamed x13 -> x1, local copies, waits for them, and re-layouts: 5.56 us -> 1.67 us
where the time goes in v2:
time: 53.9 us; the launch traced here: 53.7 us
  Pallas kernels  52.1 us (97%)
  local copies, waits for them, and re-layouts  1.67 us (3%)
    pallas_call x1, Pallas kernels, body(): pl.pallas_call(kernel, out_shape=jax.ShapeDtypeStruct((2, 64, D), bf16),...  52.1 us
    unnamed x1, local copies, waits for them, and re-layouts  1.67 us

profile of v2, /device:TPU:1, one launch (start us, length us, event | category | flops | bytes accessed | tf_op | source)
XLA Modules:
  0.0 53.7 jit_solution(8176558291216295675)
XLA Ops:
  0.0 52.1 %conformer.1 = bf16[2,64,1024]{2,1,0:T(8,128)(2,1)} custom-call(s32[2]{0:T(128)} %len_hbm.1, bf16[2,64,1024]{2,1,0:T(8,128)(2,1)} %fr_ref.1, bf16[16,3072]{1,0:T(8,128)(2,1)} %wq_ref.1, bf16[16,1024]{1,0:T(8,128)(2,1)} %wo_ref.1, bf16[16,1024]{1,0:T(8,128)(2,1)} %wp_ref.1, f32[9,1024]{1,0:T(8,128)} %wd_hbm.1), custom_call_target="tpu_custom_call" | custom-call | tf_op jit(solution)/shard_map/conformer/pallas_call | solution.py:325
  52.1 1.7 %copy.8 = bf16[2,64,1024]{2,1,0:T(8,128)(2,1)} copy(bf16[2,64,1024]{2,1,0:T(8,128)(2,1)} %conformer.1) | data formatting | bytes 524288

commit v3 on v2

--- a/solution.py
+++ b/solution.py
@@ -15,9 +15,12 @@
 LOG2E = 1.4426950408889634
 N_SEM = 160
 WA = 128
-RING_X = 0
 RING_Y = 1
-OA_AT = 2
+O_AT = 0
+OF_AT = 1
+OXN_AT = 2
+OA_AT = 1
+PX = 1
 
 
 def norm_rows(values):
@@ -57,6 +60,30 @@
     eighth = lanes(s * 128, 128)
     part_b, part_a = lanes(c * 512, 512 - WA), lanes(c * 512 + 512 - WA, WA)
 
+    started = []
+
+    def copy(src, dst, device):
+        n = len(started)
+        made = pltpu.make_async_remote_copy(
+            src_ref=src, dst_ref=dst, send_sem=ssem.at[n], recv_sem=rsem.at[n],
+            device_id=device, device_id_type=MESH,
+        )
+        made.start()
+        started.append(made)
+        return made
+
+    def same(ref, device):
+        return copy(ref, ref, device)
+
+    def arrived(copies):
+        for one in copies:
+            one.wait_recv()
+
+    barrier = pltpu.get_barrier_semaphore()
+    peers = [at_z(k) for k in (4, -4, 3, -3, 2, -2, 1, -1)]
+    peers += [at_x(k) for k in (2, 1, 3)] + [at_s(k) for k in (4, 3, 5, 2, 6, 1, 7)]
+    for peer in peers:
+        pl.semaphore_signal(barrier, inc=1, device_id=peer, device_id_type=MESH)
     local = [(fr_ref, FH.at[:, HALO : 64 + HALO])]
     local += [
         (wq_ref.at[:, lanes(part * D + s * 128, 128)], BW.at[4, x, :, part * 128 : part * 128 + 128])
@@ -74,31 +101,7 @@
     for one in local:
         one.start()
 
-    started = []
-
-    def copy(src, dst, device):
-        n = len(started)
-        made = pltpu.make_async_remote_copy(
-            src_ref=src, dst_ref=dst, send_sem=ssem.at[n], recv_sem=rsem.at[n],
-            device_id=device, device_id_type=MESH,
-        )
-        made.start()
-        started.append(made)
-        return made
-
-    def same(ref, device):
-        return copy(ref, ref, device)
-
-    def arrived(copies):
-        for one in copies:
-            one.wait_recv()
-
-    barrier = pltpu.get_barrier_semaphore()
-    peers = [at_z(k) for k in (4, -4, 3, -3, 2, -2, 1, -1)]
-    peers += [at_x(k) for k in (2, 1, 3)] + [at_s(k) for k in (4, 3, 5, 2, 6, 1, 7)]
-    for peer in peers:
-        pl.semaphore_signal(barrier, inc=1, device_id=peer, device_id_type=MESH)
-    for one in local:
+    for one in local[1:]:
         one.wait()
     pl.semaphore_wait(barrier, len(peers))
 
@@ -158,7 +161,37 @@
         return NB.at[part, there] if part < 2 else NB.at[:, there]
 
     oa0 = across(BO.at[4, x, :, part_a]) if WA else []
-    oah, oan = [], []
+    wh = hubs(BW, slot)
+    wn = near(BW, slot)
+    ph = hubs(BP, slot_eighth)
+
+    local[0].wait()
+    NB[:, s] = norm_rows(FH[:, HALO : 64 + HALO].astype(jnp.float32)).astype(jnp.bfloat16)
+
+    def frames(k, rec):
+        return NB.at[rec, lax.rem(y + k, 4) * 2 + c]
+
+    f1 = [same(frames(0, 0), at_y(1)), same(frames(0, 1), at_y(3))]
+    f1 += [same(frames(0, 1), at_y(1)), same(frames(0, 0), at_y(3))]
+    f0 = [same(NB.at[:, s], sibling)]
+    h1 = [
+        copy(fr_ref.at[:, 64 - HALO : 64], FH.at[:, 0:HALO], at_s(1)),
+        copy(fr_ref.at[:, 0:HALO], FH.at[:, 64 + HALO : 64 + 2 * HALO], at_s(7)),
+    ]
+    pn = near(BP, slot_eighth)
+
+    arrived(wh)
+    wf = far(BW, slot)
+    arrived(ph)
+    pf = far(BP, slot_eighth)
+    arrived(wn)
+    wxn = across(BW.at[NEAR, x])
+    oh, on, of, oxn, oxf, oah, oan = [], [], [], [], [], [], []
+
+    def o_start(when):
+        if when == O_AT:
+            oh.extend(hubs(BO, slot_half))
+            on.extend(near(BO, slot_half))
 
     def oa_start(when):
         if WA and when == OA_AT:
@@ -166,53 +199,45 @@
             oah.extend(hubs(BO, slot_a))
             oan.extend(near(BO, slot_a))
 
-    wh = hubs(BW, slot)
-    wn = near(BW, slot)
-    ph = hubs(BP, slot_eighth)
-    oh = hubs(BO, slot_half)
-
-    NB[:, s] = norm_rows(FH[:, HALO : 64 + HALO].astype(jnp.float32)).astype(jnp.bfloat16)
-    f1 = ring(frames_y, at_y)
-    f0 = [same(NB.at[:, s], sibling)]
-    h1 = [
-        copy(fr_ref.at[:, 64 - HALO : 64], FH.at[:, 0:HALO], at_s(1)),
-        copy(fr_ref.at[:, 0:HALO], FH.at[:, 64 + HALO : 64 + 2 * HALO], at_s(7)),
-    ]
-
-    arrived(wh)
-    wf = far(BW, slot)
-    pn = near(BP, slot_eighth)
-    on = near(BO, slot_half)
-    arrived(wn)
-    wxn = across(BW.at[NEAR, x])
-    arrived(ph)
-    pf = far(BP, slot_eighth)
-    arrived(oh)
-    of = far(BO, slot_half)
-    oa_start(0)
-    arrived(pn)
-    pxn = across(BP.at[NEAR, x, :, eighth])
+    def of_start(when):
+        if when == OF_AT:
+            arrived(oh)
+            of.extend(far(BO, slot_half))
+
+    def oxn_start(when):
+        if when == OXN_AT:
+            arrived(on)
+            oxn.extend(ring(near_x, at_x, 0))
+
+    o_start(0)
+    arrived(f1[0:2])
+    f2 = [same(frames(3, 0), at_y(1)), same(frames(1, 1), at_y(3))]
+    if PX == 0:
+        arrived(pn)
+        pxn = across(BP.at[NEAR, x, :, eighth])
+    o_start(1)
+    of_start(0)
     arrived(wf)
     wxf = across(BW.at[FAR, x])
-    oa_start(1)
-    f2 = ring_on(frames_y, at_y, f1)
-    g1 = [same(frames_y(k, 2), sibling) for k in (1, 3)]
+    o_start(2)
+    if PX == 1:
+        arrived(pn)
+        pxn = across(BP.at[NEAR, x, :, eighth])
+    arrived(f1[2:4])
+    g1 = [same(NB.at[:, lax.rem(y + k, 4) * 2 + c], sibling) for k in (1, 3)]
     arrived(pf)
     pxf = across(BP.at[FAR, x, :, eighth])
-    arrived(on)
-    oxn = ring(near_x, at_x, RING_X)
-    arrived(of)
-    oxf = ring(far_x, at_x, RING_X)
-    k1 = [same(BO.at[:, x, :, part_b], sibling)]
-    oa_start(2)
-    arrived(pxn)
-    pyn = ring(near_y, at_y, RING_Y)
+    of_start(1)
+    oxn_start(0)
+    oa_start(1)
     arrived(f2)
-    g1 += [same(frames_y(2, 2), sibling)]
+    g1 += [same(NB.at[:, lax.rem(y + 2, 4) * 2 + c], sibling)]
     arrived(wxn)
     arrived(f0)
     arrived(g1)
     arrived(wxf)
+    of_start(2)
+    oxn_start(1)
 
     def natural(ref):
         planes = [ref[lax.rem(i - z + 20, 16)] for i in range(16)]
@@ -221,74 +246,87 @@
     weight = natural(BW)
     for rec in range(2):
         rows = NB[rec].reshape(LEN, D)
-        QKV[rec] = jnp.dot(rows, weight, preferred_element_type=jnp.float32).astype(jnp.bfloat16)
+        qkv = jnp.dot(rows, weight, preferred_element_type=jnp.float32)
+        QKV[rec, HALO : LEN + HALO] = qkv.astype(jnp.bfloat16)
+        if rec == 0:
+            arrived(pxn)
+            pyn = ring(near_y, at_y, RING_Y)
+    arrived(pxf)
+    pyf = ring(far_y, at_y, RING_Y)
+    k2 = [same(BP.at[:, :, :, eighth], sibling)]
+    oxn_start(2)
+    arrived(of)
+    oxf += ring(far_x, at_x, 0)
+    k1 = [same(BO.at[:, x, :, part_b], sibling)]
+    oaf = []
     if WA:
         arrived(oah)
         oaf = far(BO, slot_a)
-    arrived(pxf)
-    pyf = ring(far_y, at_y, RING_Y)
-    k2 = [same(BP.at[:, :, :, eighth], sibling)]
-
-    a1 = []
+
     zeros = jnp.zeros((2, HALO, HDIM), jnp.bfloat16)
-    ATT[:, 0:HALO] = zeros
-    ATT[:, LEN + HALO : LEN + 2 * HALO] = zeros
-    key_at = lax.broadcasted_iota(jnp.int32, (128, LEN), 1)
-
-    def attention(rec):
-        keep = key_at < len_ref[rec]
-        keys = QKV[rec, :, HDIM : 2 * HDIM]
-        vals = QKV[rec, :, 2 * HDIM : 3 * HDIM]
-        for part in range(4):
-            query = QKV[rec, part * 128 : part * 128 + 128, 0:HDIM]
-            scores = lax.dot_general(
-                query, keys, (((1,), (1,)), ((), ())), preferred_element_type=jnp.float32
-            )
-            scores = jnp.where(keep, scores, -1e30)
-            highest = jnp.max(scores, axis=-1, keepdims=True)
-            powers = jnp.exp2((scores - highest) * (LOG2E * HDIM**-0.5))
-            totals = jnp.sum(powers, axis=-1, keepdims=True)
-            mixed = jnp.dot(powers.astype(jnp.bfloat16), vals, preferred_element_type=jnp.float32)
-            ATT[rec, HALO + part * 128 : HALO + part * 128 + 128] = (mixed / totals).astype(
-                jnp.bfloat16
-            )
+    QKV[:, 0:HALO, 0:HDIM] = zeros
+    QKV[:, LEN + HALO : LEN + 2 * HALO, 0:HDIM] = zeros
+    tall = 64 + 2 * HALO
+    wide = 128 + 2 * HALO
+    key_at = lax.broadcasted_iota(jnp.int32, (wide // 2, LEN), 1)
+
+    def attention(k):
+        chip = lax.rem(y + k, 4)
+        for rec in range(2):
+            keep = key_at < len_ref[rec]
+            keys = QKV[rec, HALO : LEN + HALO, HDIM : 2 * HDIM]
+            vals = QKV[rec, HALO : LEN + HALO, 2 * HDIM : 3 * HDIM]
+            for part in range(2):
+                first = pl.multiple_of(chip * 128 + part * (wide // 2), 16)
+                query = QKV[rec, pl.ds(first, wide // 2), 0:HDIM]
+                scores = lax.dot_general(
+                    query, keys, (((1,), (1,)), ((), ())), preferred_element_type=jnp.float32
+                )
+                scores = jnp.where(keep, scores, -1e30)
+                highest = jnp.max(scores, axis=-1, keepdims=True)
+                powers = jnp.exp2((scores - highest) * (LOG2E * HDIM**-0.5))
+                totals = jnp.sum(powers, axis=-1, keepdims=True)
+                mixed = jnp.dot(
+                    powers.astype(jnp.bfloat16), vals, preferred_element_type=jnp.float32
+                )
+                ATT[k, rec, part * (wide // 2) : (part + 1) * (wide // 2)] = (
+                    mixed / totals
+                ).astype(jnp.bfloat16)
         made = []
-        for k in (4, 3, 5, 2, 6, 1, 7):
-            there = lax.rem(s + k, 8)
-            src = ATT.at[rec, pl.ds(pl.multiple_of(there * 64, 64), 64 + 2 * HALO)]
-            made += [copy(src, A.at[rec, :, eighth], at_s(k))]
-        A[rec, :, eighth] = ATT[rec, pl.ds(pl.multiple_of(s * 64, 64), 64 + 2 * HALO)]
+        for other in (0, 1):
+            core = lax.rem(c + other, 2)
+            rows = pl.ds(pl.multiple_of(core * 64, 64), tall)
+            if k or other:
+                device = {"seq": chip * 2 + core, "dp": d}
+                made.append(copy(ATT.at[k, :, rows], A.at[:, :, eighth], device))
+            else:
+                A[:, :, eighth] = ATT[k, :, rows]
         return made
 
-    a1 += attention(0)
-    oxn2 = ring_on(near_x, at_x, oxn, RING_X)
+    a1 = attention(2) + attention(1)
+    pyn2 = ring_on(near_y, at_y, pyn, RING_Y)
+    k2 += [same(near_y(k, 2), sibling) for k in (1, 3)]
+    a1 += attention(3) + attention(0)
+    ring_on(near_x, at_x, oxn, 0)
     k1 += [same(near_x(k, 2), sibling) for k in (1, 3)]
-    a1 += attention(1)
-    oxf2 = ring_on(far_x, at_x, oxf, RING_X)
-    k1 += [same(far_x(k, 2), sibling) for k in (1, 3)]
     if WA:
         arrived(oan)
         k1 += [same(slot_a(BO, NEAR), sibling)]
-    pyn2 = ring_on(near_y, at_y, pyn, RING_Y)
-    k2 += [same(near_y(k, 2), sibling) for k in (1, 3)]
-    arrived(oxn2)
+    pyf2 = ring_on(far_y, at_y, pyf, RING_Y)
+    k2 += [same(far_y(k, 2), sibling) for k in (1, 3)]
+    arrived(oxn[2:])
     k1 += [same(near_x(2, 2), sibling)]
-    arrived(oxf2)
+    ring_on(far_x, at_x, oxf, 0)
+    k1 += [same(far_x(k, 2), sibling) for k in (1, 3)]
+    arrived(oxf[2:])
     k1 += [same(far_x(2, 2), sibling)]
     if WA:
         arrived(oaf)
         k1 += [same(slot_a(BO, FAR), sibling)]
-    pyf2 = ring_on(far_y, at_y, pyf, RING_Y)
-    k2 += [same(far_y(k, 2), sibling) for k in (1, 3)]
-    arrived(pyn2)
-    k2 += [same(near_y(2, 2), sibling)]
-    arrived(pyf2)
-    k2 += [same(far_y(2, 2), sibling)]
     arrived(h1)
     arrived(a1)
     arrived(k1)
 
-    tall = 64 + 2 * HALO
     attended = A[...].reshape(2 * tall, D)
     projected = jnp.dot(attended, natural(BO), preferred_element_type=jnp.float32)
     resid = (FH[...].astype(jnp.float32) + projected.reshape(2, tall, D)).astype(jnp.bfloat16)
@@ -299,6 +337,10 @@
         valid = inside & (position < len_ref[rec])
         normed = jnp.where(valid, norm_rows(resid[rec].astype(jnp.float32)), 0.0)
         CV[rec] = normed.astype(jnp.bfloat16).astype(jnp.float32)
+    arrived(pyn2)
+    k2 += [same(near_y(2, 2), sibling)]
+    arrived(pyf2)
+    k2 += [same(far_y(2, 2), sibling)]
     gated = []
     for rec in range(2):
         depth = jnp.zeros((64, D), jnp.float32)
@@ -333,8 +375,8 @@
             pltpu.VMEM((16, 4, 16, 3 * HDIM), bf16),
             pltpu.VMEM((16, 4, 16, D), bf16),
             pltpu.VMEM((16, 4, 16, D), bf16),
-            pltpu.VMEM((2, LEN, 3 * HDIM), bf16),
-            pltpu.VMEM((2, LEN + 2 * HALO, HDIM), bf16),
+            pltpu.VMEM((2, LEN + 2 * HALO, 3 * HDIM), bf16),
+            pltpu.VMEM((4, 2, 128 + 2 * HALO, HDIM), bf16),
             pltpu.VMEM((2, tall, D), bf16),
             pltpu.VMEM((2, tall, D), jnp.float32),
             pltpu.VMEM((KERNEL, D), jnp.float32),

time: 53.9 us -> 52.9 us (0.981)
  Pallas kernels: 52.1 us -> 51.1 us
    pallas_call x1, Pallas kernels: 52.1 us -> 51.1 us  [body(): pl.pallas_call(kernel, out_shape=jax.ShapeDtypeStruct((2, 64, D), bf16),...]
where the time goes in v3:
time: 52.9 us; the launch traced here: 52.8 us
  Pallas kernels  51.1 us (97%)
  local copies, waits for them, and re-layouts  1.67 us (3%)
    pallas_call x1, Pallas kernels, body(): pl.pallas_call(kernel, out_shape=jax.ShapeDtypeStruct((2, 64, D), bf16),...  51.1 us
    unnamed x1, local copies, waits for them, and re-layouts  1.67 us

profile of v3, /device:TPU:1, one launch (start us, length us, event | category | flops | bytes accessed | tf_op | source)
XLA Modules:
  0.0 52.8 jit_solution(14303869217120401993)
XLA Ops:
  0.0 51.1 %conformer.1 = bf16[2,64,1024]{2,1,0:T(8,128)(2,1)} custom-call(s32[2]{0:T(128)} %len_hbm.1, bf16[2,64,1024]{2,1,0:T(8,128)(2,1)} %fr_ref.1, bf16[16,3072]{1,0:T(8,128)(2,1)} %wq_ref.1, bf16[16,1024]{1,0:T(8,128)(2,1)} %wo_ref.1, bf16[16,1024]{1,0:T(8,128)(2,1)} %wp_ref.1, f32[9,1024]{1,0:T(8,128)} %wd_hbm.1), custom_call_target="tpu_custom_call" | custom-call | tf_op jit(solution)/shard_map/conformer/pallas_call | solution.py:367
  51.1 1.7 %copy.8 = bf16[2,64,1024]{2,1,0:T(8,128)(2,1)} copy(bf16[2,64,1024]{2,1,0:T(8,128)(2,1)} %conformer.1) | data formatting | bytes 524288

commit v4 on v3

--- a/solution.py
+++ b/solution.py
@@ -16,7 +16,7 @@
 N_SEM = 160
 WA = 128
 RING_Y = 1
-O_AT = 0
+O_AT = 1
 OF_AT = 1
 OXN_AT = 2
 OA_AT = 1

time: 52.9 us -> 52.9 us (level)
  no operation moved by 1% of the time
where the time goes in v4:
time: 52.9 us; the launch traced here: 52.8 us
  Pallas kernels  51.1 us (97%)
  local copies, waits for them, and re-layouts  1.67 us (3%)
    pallas_call x1, Pallas kernels, body(): pl.pallas_call(kernel, out_shape=jax.ShapeDtypeStruct((2, 64, D), bf16),...  51.1 us
    unnamed x1, local copies, waits for them, and re-layouts  1.67 us

profile of v4, /device:TPU:1, one launch (start us, length us, event | category | flops | bytes accessed | tf_op | source)
XLA Modules:
  0.0 52.8 jit_solution(15977184927986229768)
XLA Ops:
  0.0 51.1 %conformer.1 = bf16[2,64,1024]{2,1,0:T(8,128)(2,1)} custom-call(s32[2]{0:T(128)} %len_hbm.1, bf16[2,64,1024]{2,1,0:T(8,128)(2,1)} %fr_ref.1, bf16[16,3072]{1,0:T(8,128)(2,1)} %wq_ref.1, bf16[16,1024]{1,0:T(8,128)(2,1)} %wo_ref.1, bf16[16,1024]{1,0:T(8,128)(2,1)} %wp_ref.1, f32[9,1024]{1,0:T(8,128)} %wd_hbm.1), custom_call_target="tpu_custom_call" | custom-call | tf_op jit(solution)/shard_map/conformer/pallas_call | solution.py:367
  51.1 1.7 %copy.8 = bf16[2,64,1024]{2,1,0:T(8,128)(2,1)} copy(bf16[2,64,1024]{2,1,0:T(8,128)(2,1)} %conformer.1) | data formatting | bytes 524288
